TPU v7x, 32 devices: a whole 2x2x4 slice. The times are simulated.
32 devices in a mesh: batch: 8 (over y, x, core), latent: 4 (over z).
Axes of the slice: x: 2, y: 2, z: 4, core: 2. Of those that a mesh axis runs over, the one named last changes fastest.
Arguments:
- rows: bfloat16 [4096, 2048], P('batch', 'latent'), may hold values from -8 to 8, as said below
- targets: bfloat16 [256, 2048], P('batch', 'latent'), may hold values from -16 to 16
- w_up: bfloat16 [2048, 1024], P('latent'), may hold values from -2.5 to 2.5
- bias: float32 [1024], replicated, may hold values from -3 to 3
- history: int32 [256, 512], P('batch'), may hold values from 0 to 511, as said below
- requests: int32 [64, 64], P('batch'), may hold values from -1 to 511, as said below
- upstream: bfloat16 [256, 1024], P('batch', 'latent'), may hold values from -6 to 6
Outputs:
- output: bfloat16 [256, 1024], P('batch', 'latent')
- row_grad: float32 [4096, 2048], P('batch', 'latent')
Inputs may be any that keep to these rules, and one draw needn't show every extreme that they name: `requests`: row d * 8 + o lists distinct owner-local row numbers in its first entries and -1 after them, with at least one live entry; for the last owner and for one owner drawn anew, every list is full. `history`: every entry names a live slot of its user's device. `rows`: values of order one.
All inputs are finite; a program needn't handle non-finite values.
Results may differ from a plain program's by a relative error of at most 0.012.
The roundings to bfloat16 on the way count: a program that leaves them out, or rounds other values in their place, can miss the bound.
Values may be sent and summed in bfloat16 or wider, within the bound.
No kernel may reach another device: no remote copies, remote signals or barrier semaphores. Data moves between devices by JAX's collectives and lax.ppermute only.
A program may use at most 64 MiB of HBM per device.

v0:
```python
import jax
import jax.numpy as jnp
from jax import lax
from jax.sharding import PartitionSpec as P

DL = 2048


def on_device(rows, targets, w_up, bias, history, requests, upstream):
    score_scale = DL ** (-0.5)
    owners = lax.axis_size("batch")
    capacity = requests.shape[1]
    slot_count = owners * capacity
    members = targets.shape[0]
    row_width = rows.shape[1]
    stored = rows.shape[0]
    hidden_share = upstream.shape[1]
    wanted = lax.all_to_all(requests, "batch", split_axis=0, concat_axis=0, tiled=True)
    usable = wanted >= 0
    chosen = jnp.take(rows, jnp.maximum(wanted, 0).reshape(-1), axis=0)
    chosen = jnp.where(usable.reshape(-1, 1), chosen, jnp.zeros_like(chosen))
    arrived = lax.all_to_all(
        chosen.reshape(owners, capacity, row_width),
        "batch",
        split_axis=0,
        concat_axis=0,
        tiled=True,
    )
    fetched = arrived.reshape(slot_count, row_width)
    offsets = (jnp.arange(members, dtype=jnp.int32) * slot_count)[:, None]
    segment_ids = (history + offsets).reshape(-1)

    def slot_sums(values):
        return jax.ops.segment_sum(values.reshape(-1), segment_ids, members * slot_count).reshape(
            members, slot_count
        )

    slot_scores = jnp.einsum("ud,sd->us", targets, fetched, preferred_element_type=jnp.float32)
    whole_scores = lax.psum(slot_scores, "latent")
    scores = jnp.take_along_axis(whole_scores, history, axis=1) * score_scale
    probability = jax.nn.softmax(scores, axis=1)
    weight = slot_sums(probability)
    pooled = jnp.dot(
        weight.astype(jnp.bfloat16), fetched, preferred_element_type=jnp.float32
    ).astype(jnp.bfloat16)
    partial_hidden = jnp.dot(pooled, w_up, preferred_element_type=jnp.float32)
    column = lax.axis_index("latent") * hidden_share
    hidden = lax.psum_scatter(partial_hidden, "latent", scatter_dimension=1, tiled=True)
    hidden = hidden + lax.dynamic_slice_in_dim(bias, column, hidden_share)
    activated, backward = jax.vjp(jax.nn.gelu, hidden)
    output = activated.astype(jnp.bfloat16)
    slopes = backward(upstream.astype(jnp.float32))[0].astype(jnp.bfloat16)
    slopes_full = lax.all_gather(slopes, "latent", axis=1, tiled=True)
    pooled_grad = jnp.einsum("uh,dh->ud", slopes_full, w_up, preferred_element_type=jnp.float32)
    slot_slopes = jnp.einsum(
        "ud,sd->us", pooled_grad.astype(jnp.bfloat16), fetched, preferred_element_type=jnp.float32
    )
    whole_slopes = lax.psum(slot_slopes, "latent")
    probability_grad = jnp.take_along_axis(whole_slopes, history, axis=1)
    score_grad = probability * (
        probability_grad - jnp.sum(probability * probability_grad, axis=1, keepdims=True)
    )
    weight_grad = slot_sums(score_grad)
    destination = jnp.where(usable, wanted, stored)
    slot_grad = jnp.einsum("us,ud->sd", weight, pooled_grad, precision=lax.Precision.HIGHEST)
    slot_grad = slot_grad + score_scale * jnp.einsum(
        "us,ud->sd", weight_grad, targets.astype(jnp.float32), precision=lax.Precision.HIGHEST
    )
    returned = lax.all_to_all(
        slot_grad.reshape(owners, capacity, row_width),
        "batch",
        split_axis=0,
        concat_axis=0,
        tiled=True,
    )
    summed = jax.ops.segment_sum(
        returned.reshape(-1, row_width), destination.reshape(-1), stored + 1
    )
    return (output, summed[:stored])


def solution(mesh):
    return jax.shard_map(
        on_device,
        mesh=mesh,
        in_specs=(
            P("batch", "latent"),
            P("batch", "latent"),
            P("latent", None),
            P(),
            P("batch", None),
            P("batch", None),
            P("batch", "latent"),
        ),
        out_specs=(P("batch", "latent"), P("batch", "latent")),
        check_vma=False,
    )
```

profile of v0, /device:TPU:0, one launch (start us, length us, event | category | flops | bytes accessed | tf_op | source)
XLA Modules:
  0.0 615.2 jit_solution(12138111015020188799)
XLA Ops:
  7.2 9.9 %all_to_all.22 = s32[8,1,64]{2,1,0:T(1,128)S(1)} all-to-all(s32[8,1,64]{2,1,0:T(1,128)} %bitcast.59), channel_id=1, replica_groups=mesh['batch'=8,'latent'=4] {'batch'}, dimensions={0} | all-to-all | bytes 4096 | tf_op jit(solution)/shard_map/all_to_all | solution.py:18
  17.6 0.7 reduce.3
  18.4 3.1 gather_fusion
  21.5 1.0 select_select_fusion
  22.5 3.5 all-to-all-start.1
  26.1 9.5 %all-to-all-done.1 = bf16[8,64,512]{2,1,0:T(8,128)(2,1)S(1)} async-done(((bf16[8,64,512]{2,1,0:T(8,128)(2,1)}), bf16[8,64,512]{2,1,0:T(8,128)(2,1)S(1)}, u32[]{:S(2)}, u32[]{:S(2)}) %all-to-all-start.1) | async-done | bytes 524320 | tf_op jit(solution)/shard_map/all_to_all | solution.py:22
  35.7 0.9 convolution_bitcast_fusion
  36.7 33.4 %all-reduce.3.cloned.1.call-done = f32[32,512]{1,0:T(8,128)} async-done(((f32[32,512]{1,0:T(8,128)}), f32[32,512]{1,0:T(8,128)}) %all-reduce.3.cloned.1.call-update) | async-done | bytes 65552 | tf_op jit(solution)/shard_map/psum | solution.py:39
  70.1 108.9 %gather_fusion.1 = f32[16384]{0:T(1024)S(1)} fusion(f32[32,512]{1,0:T(8,128)} %all-reduce.3.cloned.1.call-done, s32[16384]{0:T(1024)S(1)} %bitcast.45), kind=kCustom, calls=%fused_computation.clone | custom fusion | bytes 262144 | tf_op jit(solution)/shard_map/jit(take_along_axis)/gather | solution.py:40
  179.5 113.5 %scatter_custom_fusion = f32[16384]{0:T(1024)S(1)} fusion(s32[16384]{0:T(1024)S(1)} %bitcast.53, f32[16384]{0:T(1024)S(1)} %bitcast.56, f32[]{:T(128)} %constant.25.clone.1), kind=kCustom, calls=%fused_computation.46 | custom fusion | flops 16384 | bytes 65540 | tf_op jit(solution)/shard_map/scatter-add | solution.py:34
  293.0 1.1 fusion.1
  294.2 0.8 dynamic_slice.3
  295.0 18.2 %reduce-scatter.2.cloned.1.call-done = f32[32,256]{1,0:T(8,128)} async-done(((f32[32,1024]{1,0:T(8,128)}), f32[32,256]{1,0:T(8,128)}) %reduce-scatter.2.cloned.1.call-update) | async-done | bytes 32784 | tf_op jit(solution)/shard_map/reduce_scatter | solution.py:48
  313.2 1.4 fusion.10
  314.6 13.1 %all_gather.3 = bf16[32,1024]{1,0:T(8,128)(2,1)S(1)} all-gather(bf16[32,256]{1,0:T(8,128)(2,1)S(1)} %get-tuple-element.5), channel_id=1, replica_groups=mesh['batch'=8,'latent'=4] {'latent'}, dimensions={1}, use_global_device_ids=true | all-gather | bytes 81920 | tf_op jit(solution)/shard_map/all_gather | solution.py:53
  328.1 0.9 fusion.18
  329.1 1.0 fusion.27
  330.1 31.3 %all-reduce.5.cloned.1.call-done = f32[32,512]{1,0:T(8,128)} async-done(((f32[32,512]{1,0:T(8,128)}), f32[32,512]{1,0:T(8,128)}) %all-reduce.5.cloned.1.call-update) | async-done | bytes 65552 | tf_op jit(solution)/shard_map/psum | solution.py:58
  361.4 108.9 %gather_fusion.2 = f32[16384]{0:T(1024)S(1)} fusion(f32[32,512]{1,0:T(8,128)} %all-reduce.5.cloned.1.call-done, s32[16384]{0:T(1024)S(1)} %bitcast.46), kind=kCustom, calls=%fused_computation.1.clone | custom fusion | bytes 262144 | tf_op jit(solution)/shard_map/jit(take_along_axis)/gather | solution.py:59
  470.6 113.5 %scatter_custom_fusion.1 = f32[16384]{0:T(1024)S(1)} fusion(s32[16384]{0:T(1024)S(1)} %bitcast.54, f32[16384]{0:T(1024)S(1)} %bitcast.55, f32[]{:T(128)} %constant.25.clone.1), kind=kCustom, calls=%fused_computation.44 | custom fusion | flops 16384 | bytes 65540 | tf_op jit(solution)/shard_map/scatter-add | solution.py:34
  584.2 0.7 fusion
  584.8 18.8 %all_to_all.23 = f32[8,64,512]{2,1,0:T(8,128)S(1)} all-to-all(f32[8,64,512]{2,1,0:T(8,128)S(1)} %bitcast.50), channel_id=1, replica_groups=mesh['batch'=8,'latent'=4] {'batch'}, dimensions={0} | all-to-all | bytes 2097152 | tf_op jit(solution)/shard_map/all_to_all | solution.py:69
  603.6 4.0 scatter_custom_fusion.2
  607.6 1.0 slice.10
  (38 shorter events, 2.2 us)
Async XLA Ops:
  7.2 285.9 %copy-start = (bf16[512,1024]{1,0:T(8,128)(2,1)S(1)}, bf16[512,1024]{1,0:T(8,128)(2,1)}, u32[]{:S(2)}) copy-start(bf16[512,1024]{1,0:T(8,128)(2,1)} %param.11) | copy-start | bytes 3145732
  21.5 4.6 copy-start.1
  21.5 14.2 %copy-start.2 = (bf16[32,512]{1,0:T(8,128)(2,1)S(1)}, bf16[32,512]{1,0:T(8,128)(2,1)}, u32[]{:S(2)}) copy-start(bf16[32,512]{1,0:T(8,128)(2,1)} %param.10) | copy-start | bytes 98308
  22.5 13.2 %all-to-all-start.1 = ((bf16[8,64,512]{2,1,0:T(8,128)(2,1)}), bf16[8,64,512]{2,1,0:T(8,128)(2,1)S(1)}, u32[]{:S(2)}, u32[]{:S(2)}) async-start(bf16[8,64,512]{2,1,0:T(8,128)(2,1)} %select_select_fusion), calls=%async_computation.1 | async-start | bytes 1048576 | tf_op jit(solution)/shard_map/all_to_all | solution.py:22
  26.0 44.1 %all-reduce.3.cloned.1.call-start = ((), (), s32[]{:S(2)}) async-start(), calls=%async_computation.4 | async-start | bytes 131072 | tf_op jit(solution)/shard_map/psum | solution.py:39
  36.6 276.6 %reduce-scatter.2.cloned.1.call-start = ((), (), s32[]{:S(2)}) async-start(), calls=%async_computation.5 | async-start | bytes 163840 | tf_op jit(solution)/shard_map/reduce_scatter | solution.py:48
  293.0 20.2 %copy-start.3 = (bf16[32,256]{1,0:T(8,128)(2,1)S(1)}, bf16[32,256]{1,0:T(8,128)(2,1)}, u32[]{:S(2)}) copy-start(bf16[32,256]{1,0:T(8,128)(2,1)} %param.15) | copy-start | bytes 49156
  294.2 67.2 %all-reduce.5.cloned.1.call-start = ((), (), s32[]{:S(2)}) async-start(), calls=%async_computation.6 | async-start | bytes 131072 | tf_op jit(solution)/shard_map/psum | solution.py:58
Sparse Core Ops, SparseCore 0:
  36.7 33.3 all-reduce.2
  294.3 18.8 reduce-scatter.1
  329.2 32.1 all-reduce.4
where the time goes:
time: 616 us; the launch traced here: 615 us
  other arithmetic  235 us (38%)
  local copies, waits for them, and re-layouts  223 us (36%)
  waiting for transfers between devices  92.5 us (15%)
  blocking collectives  41.8 us (7%)
  between operations  14 us (2%)
    scatter-add x2, other arithmetic, slot_sums(): jax.ops.segment_sum(values.reshape(-1), segment_ids, members * slot_count)  227 us
    gather x2, local copies, waits for them, and re-layouts, on_device(): scores = jnp.take_along_axis(whole_scores, history, axis=1) * score_scale  109 us
    gather x2, local copies, waits for them, and re-layouts, on_device(): probability_grad = jnp.take_along_axis(whole_slopes, history, axis=1)  109 us
    psum x1, waiting for transfers between devices, on_device(): whole_scores = lax.psum(slot_scores, 'latent')  33.4 us
    psum x1, waiting for transfers between devices, on_device(): whole_slopes = lax.psum(slot_slopes, 'latent')  31.3 us
    all_to_all x1, blocking collectives, on_device(): lax.all_to_all(slot_grad.reshape(owners, capacity, row_width), 'batch', s...  18.8 us
    reduce_scatter x1, waiting for transfers between devices, on_device(): lax.psum_scatter(partial_hidden, 'latent', scatter_dimension=1, tiled=True)  18.2 us
    all_gather x1, blocking collectives, on_device(): slopes_full = lax.all_gather(slopes, 'latent', axis=1, tiled=True)  13.1 us
  transfers between devices with their start and end apart: 4, of which 4 were waited for; matrix products, arithmetic and copies ran while one was open for 0% of the time, Pallas kernels for 0%

commit v1 on v0

--- a/solution.py
+++ b/solution.py
@@ -2,8 +2,19 @@
 import jax.numpy as jnp
 from jax import lax
 from jax.sharding import PartitionSpec as P
+from jax.lax import axis_size, ppermute
 
 DL = 2048
+
+
+def push_the_cube(own_rows):
+    row_axis = "latent"
+    chips = axis_size(row_axis)
+    shaped = lambda w_next: [(idx, idx ^ w_next) for idx in range(chips)]
+    block_now = own_rows
+    for dd in range(chips.bit_length() - 1):
+        block_now = block_now + ppermute(block_now, row_axis, shaped(1 << dd))
+    return block_now
 
 
 def on_device(rows, targets, w_up, bias, history, requests, upstream):
@@ -55,7 +66,7 @@
     slot_slopes = jnp.einsum(
         "ud,sd->us", pooled_grad.astype(jnp.bfloat16), fetched, preferred_element_type=jnp.float32
     )
-    whole_slopes = lax.psum(slot_slopes, "latent")
+    whole_slopes = push_the_cube(slot_slopes)
     probability_grad = jnp.take_along_axis(whole_slopes, history, axis=1)
     score_grad = probability * (
         probability_grad - jnp.sum(probability * probability_grad, axis=1, keepdims=True)

time: 616 us -> 613 us (level)
  waiting for transfers between devices: 92.5 us -> 69.2 us
  local copies, waits for them, and re-layouts: 223 us -> 244 us
    psum x1 -> x0, waiting for transfers between devices: 31.3 us -> none  [on_device(): whole_slopes = lax.psum(slot_slopes, 'latent')]
    gather x2, local copies, waits for them, and re-layouts: 109 us -> 129 us  [on_device(): probability_grad = jnp.take_along_axis(whole_slopes, history, axis=1)]
    ppermute x0 -> x2, waiting for transfers between devices: none -> 7.94 us  [push_the_cube(): block_now = block_now + ppermute(block_now, row_axis, shaped(1 << dd))]
  transfers between devices with their start and end apart: 4 -> 5, of which waited for: 4 -> 5; matrix products, arithmetic and copies ran while one was open for 0% -> 0% of each run, Pallas kernels for 0% -> 0%
where the time goes in v1:
time: 613 us
  local copies, waits for them, and re-layouts  244 us (40%)
  other arithmetic  235 us (38%)
  waiting for transfers between devices  69.2 us (11%)
  blocking collectives  41.8 us (7%)
  between operations  14.3 us (2%)
    scatter-add x2, other arithmetic, slot_sums(): jax.ops.segment_sum(values.reshape(-1), segment_ids, members * slot_count)  227 us
    gather x2, local copies, waits for them, and re-layouts, on_device(): probability_grad = jnp.take_along_axis(whole_slopes, history, axis=1)  129 us
    gather x2, local copies, waits for them, and re-layouts, on_device(): scores = jnp.take_along_axis(whole_scores, history, axis=1) * score_scale  109 us
    psum x1, waiting for transfers between devices, on_device(): whole_scores = lax.psum(slot_scores, 'latent')  33.4 us
    all_to_all x1, blocking collectives, on_device(): lax.all_to_all(slot_grad.reshape(owners, capacity, row_width), 'batch', s...  18.8 us
    reduce_scatter x1, waiting for transfers between devices, on_device(): lax.psum_scatter(partial_hidden, 'latent', scatter_dimension=1, tiled=True)  18.3 us
    all_gather x1, blocking collectives, on_device(): slopes_full = lax.all_gather(slopes, 'latent', axis=1, tiled=True)  13.1 us
  transfers between devices with their start and end apart: 5, of which 5 were waited for; matrix products, arithmetic and copies ran while one was open for 0% of the time, Pallas kernels for 0%

profile of v1, /device:TPU:0, one launch (start us, length us, event | category | flops | bytes accessed | tf_op | source)
XLA Modules:
  0.0 612.8 jit_solution(4246375329917608825)
XLA Ops:
  7.2 9.9 %all_to_all.22 = s32[8,1,64]{2,1,0:T(1,128)S(1)} all-to-all(s32[8,1,64]{2,1,0:T(1,128)} %bitcast.59), channel_id=1, replica_groups=mesh['batch'=8,'latent'=4] {'batch'}, dimensions={0} | all-to-all | bytes 4096 | tf_op jit(solution)/shard_map/all_to_all | solution.py:29
  17.6 0.7 reduce.3
  18.4 3.1 gather_fusion
  21.5 1.0 select_select_fusion
  22.5 3.5 all-to-all-start.1
  26.1 9.5 %all-to-all-done.1 = bf16[8,64,512]{2,1,0:T(8,128)(2,1)S(1)} async-done(((bf16[8,64,512]{2,1,0:T(8,128)(2,1)}), bf16[8,64,512]{2,1,0:T(8,128)(2,1)S(1)}, u32[]{:S(2)}, u32[]{:S(2)}) %all-to-all-start.1) | async-done | bytes 524320 | tf_op jit(solution)/shard_map/all_to_all | solution.py:33
  35.7 0.9 convolution_bitcast_fusion
  36.7 33.4 %all-reduce.2.cloned.1.call-done = f32[32,512]{1,0:T(8,128)} async-done(((f32[32,512]{1,0:T(8,128)}), f32[32,512]{1,0:T(8,128)}) %all-reduce.2.cloned.1.call-update) | async-done | bytes 65552 | tf_op jit(solution)/shard_map/psum | solution.py:50
  70.1 108.9 %gather_fusion.1 = f32[16384]{0:T(1024)S(1)} fusion(f32[32,512]{1,0:T(8,128)} %all-reduce.2.cloned.1.call-done, s32[16384]{0:T(1024)S(1)} %bitcast.45), kind=kCustom, calls=%fused_computation.clone | custom fusion | bytes 262144 | tf_op jit(solution)/shard_map/jit(take_along_axis)/gather | solution.py:51
  179.5 113.5 %scatter_custom_fusion = f32[16384]{0:T(1024)S(1)} fusion(s32[16384]{0:T(1024)S(1)} %bitcast.53, f32[16384]{0:T(1024)S(1)} %bitcast.56, f32[]{:T(128)} %constant.25.clone.1), kind=kCustom, calls=%fused_computation.46 | custom fusion | flops 16384 | bytes 65540 | tf_op jit(solution)/shard_map/scatter-add | solution.py:45
  293.0 1.1 fusion.1
  294.2 0.8 dynamic_slice.3
  294.9 18.3 %reduce-scatter.2.cloned.1.call-done = f32[32,256]{1,0:T(8,128)} async-done(((f32[32,1024]{1,0:T(8,128)}), f32[32,256]{1,0:T(8,128)}) %reduce-scatter.2.cloned.1.call-update) | async-done | bytes 32784 | tf_op jit(solution)/shard_map/reduce_scatter | solution.py:59
  313.2 1.4 fusion.10
  314.6 13.1 %all_gather.3 = bf16[32,1024]{1,0:T(8,128)(2,1)S(1)} all-gather(bf16[32,256]{1,0:T(8,128)(2,1)S(1)} %get-tuple-element.5), channel_id=1, replica_groups=mesh['batch'=8,'latent'=4] {'latent'}, dimensions={1}, use_global_device_ids=true | all-gather | bytes 81920 | tf_op jit(solution)/shard_map/all_gather | solution.py:64
  328.4 4.2 collective-permute-done
  333.4 1.0 fusion.27
  334.4 3.7 collective-permute-done.1
  338.1 129.5 %gather_fusion.2 = f32[16384]{0:T(1024)S(1)} fusion(f32[32,512]{1,0:T(8,128)S(1)} %add.66, s32[16384]{0:T(1024)S(1)} %bitcast.46), kind=kCustom, calls=%fused_computation.1.clone | custom fusion | bytes 262144 | tf_op jit(solution)/shard_map/jit(take_along_axis)/gather | solution.py:70
  467.9 113.5 %scatter_custom_fusion.1 = f32[16384]{0:T(1024)S(1)} fusion(s32[16384]{0:T(1024)S(1)} %bitcast.54, f32[16384]{0:T(1024)S(1)} %bitcast.55, f32[]{:T(128)} %constant.25.clone.1), kind=kCustom, calls=%fused_computation.44 | custom fusion | flops 16384 | bytes 65540 | tf_op jit(solution)/shard_map/scatter-add | solution.py:45
  581.4 0.7 fusion
  582.1 18.8 %all_to_all.23 = f32[8,64,512]{2,1,0:T(8,128)S(1)} all-to-all(f32[8,64,512]{2,1,0:T(8,128)S(1)} %bitcast.50), channel_id=1, replica_groups=mesh['batch'=8,'latent'=4] {'batch'}, dimensions={0} | all-to-all | bytes 2097152 | tf_op jit(solution)/shard_map/all_to_all | solution.py:80
  600.9 4.0 scatter_custom_fusion.2
  604.9 1.0 slice.10
  (41 shorter events, 3.1 us)
Async XLA Ops:
  7.2 285.9 %copy-start = (bf16[512,1024]{1,0:T(8,128)(2,1)S(1)}, bf16[512,1024]{1,0:T(8,128)(2,1)}, u32[]{:S(2)}) copy-start(bf16[512,1024]{1,0:T(8,128)(2,1)} %param.11) | copy-start | bytes 3145732
  21.5 4.6 copy-start.1
  21.5 14.2 %copy-start.2 = (bf16[32,512]{1,0:T(8,128)(2,1)S(1)}, bf16[32,512]{1,0:T(8,128)(2,1)}, u32[]{:S(2)}) copy-start(bf16[32,512]{1,0:T(8,128)(2,1)} %param.10) | copy-start | bytes 98308
  22.5 13.2 %all-to-all-start.1 = ((bf16[8,64,512]{2,1,0:T(8,128)(2,1)}), bf16[8,64,512]{2,1,0:T(8,128)(2,1)S(1)}, u32[]{:S(2)}, u32[]{:S(2)}) async-start(bf16[8,64,512]{2,1,0:T(8,128)(2,1)} %select_select_fusion), calls=%async_computation.1 | async-start | bytes 1048576 | tf_op jit(solution)/shard_map/all_to_all | solution.py:33
  26.0 44.1 %all-reduce.2.cloned.1.call-start = ((), (), s32[]{:S(2)}) async-start(), calls=%async_computation.4 | async-start | bytes 131072 | tf_op jit(solution)/shard_map/psum | solution.py:50
  36.6 276.6 %reduce-scatter.2.cloned.1.call-start = ((), (), s32[]{:S(2)}) async-start(), calls=%async_computation.5 | async-start | bytes 163840 | tf_op jit(solution)/shard_map/reduce_scatter | solution.py:59
  179.5 133.8 %copy-start.3 = (bf16[32,256]{1,0:T(8,128)(2,1)S(1)}, bf16[32,256]{1,0:T(8,128)(2,1)}, u32[]{:S(2)}) copy-start(bf16[32,256]{1,0:T(8,128)(2,1)} %param.15) | copy-start | bytes 49156
  328.4 4.3 collective-permute-start
  332.7 5.4 collective-permute-start.1
Sparse Core Ops, SparseCore 0:
  36.7 33.3 all-reduce.1
  294.3 18.8 reduce-scatter.1
